TPU v7x, 256 devices: a whole 4x4x8 slice. The times are simulated.
256 devices in a mesh: grp: 16 (over x, z_hi), rep: 16 (over y, z_lo, core).
Axes of the slice: x: 4, y: 4, z: 8 (z_hi: 4, z_lo: 2; z = z_hi * 2 + z_lo), core: 2. Of those that a mesh axis runs over, the one named last changes fastest.
Arguments:
- trainer_gate: bfloat16 [6, 7168, 2048], P(None, ('rep', 'grp')), may hold values from -1 to 1
- expert_of_slot: int32 [6], replicated, may hold values from 0 to 5, each once
Outputs:
- rollout_gate: bfloat16 [6, 7168, 2048], P(None, None, 'grp')
- block_scales: bfloat16 [6, 56, 16], P(None, None, 'grp')
All inputs are finite; a program needn't handle non-finite values.
Results may differ from a plain program's by a relative error of at most 0.0014.
Values may be sent and summed in bfloat16 or wider, within the bound.
A program may use at most 128 MiB of HBM per device.

v0:
```python
import jax
import jax.numpy as jnp
from jax import lax
from jax.sharding import PartitionSpec as P

QB = 128
QC = 128


def quantize(source):
    count, rows, width = source.shape
    blocks = source.astype(jnp.float32).reshape(count, rows // QB, QB, width // QC, QC)
    largest = jnp.max(jnp.abs(blocks), axis=(2, 4)) + 1e-06
    scales = largest.astype(jnp.bfloat16)
    divisor = scales.astype(jnp.float32)[:, :, None, :, None]
    scaled = (blocks / divisor).astype(jnp.bfloat16).reshape(count, rows, width)
    return (scaled, scales)


def shards(trainer_gate, expert_of_slot):
    placed = jnp.take(trainer_gate, expert_of_slot, axis=0)
    local = lax.all_to_all(placed, "grp", split_axis=2, concat_axis=1, tiled=True)
    collected = lax.all_gather(local, "rep", axis=1, tiled=True)
    scaled, scales = quantize(collected)
    return (scaled, scales)


def solution(mesh):
    return jax.shard_map(
        shards,
        mesh=mesh,
        in_specs=(P(None, ("rep", "grp"), None), P()),
        out_specs=(P(None, None, "grp"), P(None, None, "grp")),
        check_vma=False,
    )
```

profile of v0, /device:TPU:1, one launch (start us, length us, event | category | flops | bytes accessed | tf_op | source)
XLA Modules:
  0.0 151.1 jit_solution(9555283939964291719)
XLA Ops:
  7.2 0.0 copy-start
  7.2 0.0 all-gather.2.cloned.1.call-start
  7.2 0.7 compare_and_fusion
  8.0 0.7 compare_select_fusion
  8.6 0.0 copy-done
  8.6 0.6 gather_fusion
  9.2 0.1 broadcast_select_fusion
  9.4 4.2 %copy.9 = bf16[6,28,2048]{1,0,2:T(8,128)(2,1)} copy(bf16[6,28,2048]{2,1,0:T(8,128)(2,1)S(1)} %broadcast_select_fusion) | data formatting | bytes 1376256 | tf_op jit(solution)/shard_map/jit(_take)/select_n | solution.py:21
  13.5 5.8 %reshape.54 = bf16[16,2,10752]{2,1,0:T(2,128)(2,1)S(1)} reshape(bf16[2048,6,28]{2,1,0:T(8,128)(2,1)} %bitcast.14) | data formatting | bytes 1376256
  19.3 31.7 %all_to_all.18 = bf16[16,2,10752]{2,1,0:T(2,128)(2,1)S(1)} all-to-all(bf16[16,2,10752]{2,1,0:T(2,128)(2,1)S(1)} %reshape.54), channel_id=1, replica_groups=mesh['grp'=16,'rep'=16] {'grp'}, dimensions={0} | all-to-all | bytes 1376256 | tf_op jit(solution)/shard_map/all_to_all | solution.py:22
  51.1 5.9 %reshape.55 = bf16[2048,6,28]{2,1,0:T(8,128)(2,1)} reshape(bf16[16,2,10752]{2,1,0:T(2,128)(2,1)S(1)} %all_to_all.18) | data formatting | bytes 1376256
  57.0 4.4 %copy.10 = bf16[6,28,16,128]{3,1,2,0:T(8,128)(2,1)S(1)} copy(bf16[6,28,16,128]{1,0,3,2:T(8,128)(2,1)} %bitcast.15) | data formatting | bytes 1376256 | tf_op jit(solution)/shard_map/all_to_all | solution.py:22
  61.4 1.0 all_to_all.16
  62.4 0.0 all-gather.2.cloned.1.call-update
  62.4 65.3 %all-gather.2.cloned.1.call-done = bf16[6,7168,128]{2,1,0:T(8,128)(2,1)} async-done(((bf16[6,448,128]{2,1,0:T(8,128)(2,1)}), bf16[6,7168,128]{2,1,0:T(8,128)(2,1)}) %all-gather.2.cloned.1.call-update) | async-done | bytes 11010064 | tf_op jit(solution)/shard_map/all_gather | solution.py:23
  127.7 0.0 copy-start.1
  127.7 7.9 %fusion = f32[6,7168]{1,0:T(8,128)S(1)} fusion(bf16[6,7168,128]{2,1,0:T(8,128)(2,1)} %all-gather.2.cloned.1.call-done), kind=kLoop, calls=%fused_computation.3 | loop fusion | flops 16472064 | bytes 11182080 | tf_op jit(solution)/shard_map/reduce_max | solution.py:13
  135.6 0.1 bitcast_reduce_fusion
  135.7 0.6 fusion.2
  136.3 0.1 broadcast_bitcast_fusion
  136.5 0.0 copy-done.1
  136.5 7.8 %fusion.1 = bf16[6,7168,128]{2,1,0:T(8,128)(2,1)} fusion(bf16[6,7168,128]{2,1,0:T(8,128)(2,1)S(1)} %copy-done.1, f32[6,7168]{1,0:T(8,128)S(1)} %bitcast.17), kind=kLoop, calls=%fused_computation.4 | loop fusion | flops 16515072 | bytes 22192128 | tf_op jit(solution)/shard_map/convert_element_type | solution.py:16
  (2 shorter events, 0.1 us)
Async XLA Ops:
  7.2 1.5 copy-start
  7.2 120.5 %all-gather.2.cloned.1.call-start = ((), (), s32[]{:S(2)}) async-start(), calls=%async_computation.1 | async-start | bytes 11698176 | tf_op jit(solution)/shard_map/all_gather | solution.py:23
  127.7 8.8 %copy-start.1 = (bf16[6,7168,128]{2,1,0:T(8,128)(2,1)S(1)}, bf16[6,7168,128]{2,1,0:T(8,128)(2,1)}, u32[]{:S(2)}) copy-start(bf16[6,7168,128]{2,1,0:T(8,128)(2,1)} %all-gather.2.cloned.1.call-done) | copy-start | bytes 33030148
Sparse Core Ops, SparseCore 0:
  62.6 65.0 all-gather.1
where the time goes:
time: 151 us
  waiting for transfers between devices  65.3 us (43%)
  blocking collectives  31.7 us (21%)
  local copies, waits for them, and re-layouts  22 us (15%)
  other arithmetic  17.9 us (12%)
  between operations  14.1 us (9%)
    all_gather x1, waiting for transfers between devices, shards(): collected = lax.all_gather(local, 'rep', axis=1, tiled=True)  65.3 us
    all_to_all x1, blocking collectives, shards(): lax.all_to_all(placed, 'grp', split_axis=2, concat_axis=1, tiled=True)  31.7 us
    unnamed x8, local copies, waits for them, and re-layouts  11.9 us
    reduce_max x2, other arithmetic, quantize(): largest = jnp.max(jnp.abs(blocks), axis=(2, 4)) + 1e-06  8.01 us
    convert_element_type x1, other arithmetic, quantize(): scaled = (blocks / divisor).astype(jnp.bfloat16).reshape(count, rows, width)  7.76 us
    all_to_all x2, local copies, waits for them, and re-layouts, shards(): lax.all_to_all(placed, 'grp', split_axis=2, concat_axis=1, tiled=True)  5.43 us
    select_n x1, local copies, waits for them, and re-layouts, shards(): placed = jnp.take(trainer_gate, expert_of_slot, axis=0)  4.16 us
  transfers between devices with their start and end apart: 1, of which 1 were waited for; matrix products, arithmetic and copies ran while one was open for 0% of the time, Pallas kernels for 0%

commit v1 on v0

v1 whole, which is shorter than its diff:
```python
import functools

import jax
import jax.numpy as jnp
from jax import lax
from jax.experimental import pallas as pl
from jax.experimental.pallas import tpu as pltpu
from jax.sharding import PartitionSpec as P

MESH = pl.DeviceIdType.MESH
EXPERTS, ROWS, FF = 6, 28, 2048
QB = 128
NX, NZ, NY = 4, 4, 4
CHUNKS = 3
SOURCES = 32
SHARE = SOURCES * ROWS
BLOCKS = SHARE // QB
FULL = SHARE + 16
CHIPS = 8

H1 = (0, 448)
H2 = (448, FULL - 448)
A1 = (0, 336)
A2 = (560, FULL - 560)
B = (336, 224)
ALL = (0, FULL)
TAGS = 32


def spread(x_ref, buf, xv, got, rows, load_sem, own_sem, out_sem, in_sem, ssem, rsem):
    g, r = lax.axis_index("grp"), lax.axis_index("rep")
    x, zh = g // NZ, g % NZ
    y, z, c = r // 4, (r // 2) % 2, r % 2

    load = pltpu.make_async_copy(x_ref, xv, load_sem)
    load.start()

    def at(gx, gz, yy, zz, cc):
        return (gx * NZ + gz, (yy * 2 + zz) * 2 + cc)

    up = at(x, zh, (y + 1) % NY, z, c)
    down = at(x, zh, (y + 3) % NY, z, c)
    side = at(x, zh, y, 1 - z, c)
    twin = at(x, zh, y, z, 1 - c)
    exchange = [
        (dx, dz, fc) for dz in (2, 1, 3, 0) for dx in (2, 1, 3, 0) for fc in (0, 1) if (dx, dz, fc) != (0, 0, 0)
    ]

    def peer(dx, dz, fc):
        return (x + dx) % NX, (zh + dz) % NZ, (c + fc) % 2

    barrier = pltpu.get_barrier_semaphore()
    for p in exchange:
        gx, gz, cc = peer(*p)
        pl.semaphore_signal(barrier, inc=1, device_id=at(gx, gz, y, z, cc), device_id_type=MESH)
    for d in (up, down, side):
        pl.semaphore_signal(barrier, inc=1, device_id=d, device_id_type=MESH)
    load.wait()
    mine = c * 16 + g
    for k in range(CHUNKS):
        pltpu.make_async_copy(
            xv.at[c * CHUNKS + k, :, pl.ds(pl.multiple_of(g * QB, QB), QB)], got.at[k, mine], own_sem.at[k]
        ).start()
    pl.semaphore_wait(barrier, len(exchange) + 3)

    for k in range(CHUNKS):
        for p in exchange:
            gx, gz, cc = peer(*p)
            col = pl.multiple_of((gx * NZ + gz) * QB, QB)
            pltpu.make_async_remote_copy(
                src_ref=xv.at[cc * CHUNKS + k, :, pl.ds(col, QB)],
                dst_ref=got.at[k, mine],
                send_sem=out_sem.at[k],
                recv_sem=in_sem.at[k],
                device_id=at(gx, gz, y, z, cc),
                device_id_type=MESH,
            ).start()

    def chip(dy, dz):
        return ((y + dy) % NY) * 2 + (z + dz) % 2

    def copy(k, tag, origin, piece, target, fc=0):
        e = (c + fc) % 2 * CHUNKS + k
        part = buf.at[e, origin, pl.ds(piece[0], piece[1])]
        return pltpu.make_async_remote_copy(
            src_ref=part,
            dst_ref=part,
            send_sem=ssem.at[k, tag],
            recv_sem=rsem.at[k, tag],
            device_id=target,
            device_id_type=MESH,
        )

    plan = {
        0: (chip(0, 0), H1, up),
        1: (chip(0, 0), H2, up),
        2: (chip(0, 0), H2, down),
        3: (chip(0, 0), H1, down),
        4: (chip(0, 0), A1, side),
        5: (chip(0, 0), A2, side),
        6: (chip(0, 0), B, side),
        7: (chip(3, 0), H1, up),
        8: (chip(1, 0), H2, down),
        9: (chip(0, 1), A1, up),
        10: (chip(0, 1), A2, up),
        11: (chip(0, 1), A2, down),
        12: (chip(0, 1), A1, down),
        13: (chip(3, 1), A1, up),
        14: (chip(1, 1), A2, down),
        15: (chip(3, 0), B, side),
        16: (chip(1, 0), B, side),
        17: (chip(2, 0), B, side),
        18: (chip(0, 0), ALL, twin),
        19: (chip(0, 1), ALL, twin),
        20: (chip(3, 0), ALL, twin),
        21: (chip(1, 0), ALL, twin),
        22: (chip(2, 0), ALL, twin),
        23: (chip(3, 1), A1, twin),
        24: (chip(3, 1), A2, twin),
        25: (chip(1, 1), A2, twin),
        26: (chip(1, 1), A1, twin),
        27: (chip(2, 1), A1, twin),
        28: (chip(2, 1), A2, twin),
        29: (chip(3, 1), B, twin),
        30: (chip(1, 1), B, twin),
        31: (chip(2, 1), B, twin),
    }
    came = {
        0: chip(3, 0), 1: chip(3, 0), 2: chip(1, 0), 3: chip(1, 0),
        4: chip(0, 1), 5: chip(0, 1), 6: chip(0, 1),
        7: chip(2, 0), 8: chip(2, 0),
        9: chip(3, 1), 10: chip(3, 1), 11: chip(1, 1), 12: chip(1, 1),
        13: chip(2, 1), 14: chip(2, 1),
        15: chip(3, 1), 16: chip(1, 1), 17: chip(2, 1),
    }

    def send(k, *tags):
        for t in tags:
            copy(k, t, *plan[t]).start()

    def wait(k, *tags):
        for t in tags:
            if t < 18:
                copy(k, t, came[t], plan[t][1], plan[t][2]).wait_recv()
            else:
                copy(k, t, plan[t][0], plan[t][1], plan[t][2], 1).wait_recv()

    def scale(k):
        e, here = c * CHUNKS + k, chip(0, 0)
        pltpu.make_async_copy(got.at[k, 0], got.at[k, 0], own_sem.at[k]).wait()
        pltpu.make_async_copy(got.at[k, pl.ds(0, SOURCES - 1)], got.at[k, pl.ds(0, SOURCES - 1)], in_sem.at[k]).wait()
        for j in range(SOURCES):
            rows[pl.ds(j * ROWS, ROWS), :] = got[k, j].astype(jnp.float32)
        row = lax.broadcasted_iota(jnp.int32, (16, QB), 0)
        scales = jnp.zeros((16, QB), jnp.float32)
        for b in range(BLOCKS):
            v = rows[pl.ds(b * QB, QB), :]
            m = jnp.max(jnp.max(jnp.abs(v), axis=0, keepdims=True), axis=1, keepdims=True) + 1e-06
            s = jnp.broadcast_to(m, (16, QB)).astype(jnp.bfloat16).astype(jnp.float32)
            buf[e, here, pl.ds(b * QB, QB), :] = (v / s[0:1]).astype(jnp.bfloat16)
            scales = jnp.where(row == b, s, scales)
        buf[e, here, pl.ds(SHARE, 16), :] = scales.astype(jnp.bfloat16)
        send(k, 0, 2, 4, 5, 1, 3, 6, 18)

    def early(k):
        wait(k, 0)
        send(k, 7)
        wait(k, 2)
        send(k, 8)
        wait(k, 4)
        send(k, 9, 12)
        wait(k, 5)
        send(k, 11, 10)
        wait(k, 1)
        send(k, 15, 20)
        wait(k, 3)
        send(k, 16, 21)
        wait(k, 6)
        send(k, 19)
        wait(k, 7, 8)
        send(k, 17, 22)

    def late(k):
        wait(k, 9)
        send(k, 13, 23)
        wait(k, 11)
        send(k, 14, 25)
        wait(k, 10)
        send(k, 24)
        wait(k, 12)
        send(k, 26)
        wait(k, 15)
        send(k, 29)
        wait(k, 16)
        send(k, 30)
        wait(k, 13)
        send(k, 27)
        wait(k, 14)
        send(k, 28)
        wait(k, 17)
        send(k, 31)

    scale(0)
    early(0)
    scale(1)
    late(0)
    early(1)
    scale(2)
    late(1)
    early(2)
    late(2)
    for k in range(CHUNKS):
        for t in range(18, TAGS):
            wait(k, t)
        for t in range(TAGS):
            copy(k, t, *plan[t]).wait_send()
        pltpu.make_async_copy(got.at[k, pl.ds(0, SOURCES - 1)], got.at[k, pl.ds(0, SOURCES - 1)], out_sem.at[k]).wait()


def place(slot_ref, buf, out_ref, scale_ref, sem):
    for s in range(EXPERTS):
        e = slot_ref[s]
        for ch in range(CHIPS):
            pltpu.make_async_copy(
                buf.at[e, ch, pl.ds(0, SHARE)], out_ref.at[s, pl.ds(ch * SHARE, SHARE)], sem.at[s, ch]
            ).start()
    for s in range(EXPERTS):
        e = slot_ref[s]
        parts = [buf[e, ch, pl.ds(SHARE, 16), :].astype(jnp.float32)[:BLOCKS] for ch in range(CHIPS)]
        scale_ref[s] = jnp.concatenate(parts, axis=0)[:, 0:1].astype(jnp.bfloat16)
    for s in range(EXPERTS):
        for ch in range(CHIPS):
            pltpu.make_async_copy(
                buf.at[0, ch, pl.ds(0, SHARE)], out_ref.at[s, pl.ds(ch * SHARE, SHARE)], sem.at[s, ch]
            ).wait()


def shards(trainer_gate, expert_of_slot):
    gathered = pl.pallas_call(
        spread,
        out_shape=pltpu.VMEM((EXPERTS, CHIPS, FULL, QB), jnp.bfloat16),
        in_specs=[pl.BlockSpec(memory_space=pl.ANY)],
        out_specs=pl.BlockSpec(memory_space=pltpu.VMEM),
        scratch_shapes=[
            pltpu.VMEM((EXPERTS, ROWS, FF), jnp.bfloat16),
            pltpu.VMEM((CHUNKS, SOURCES, ROWS, QB), jnp.bfloat16),
            pltpu.VMEM((SHARE, QB), jnp.float32),
            pltpu.SemaphoreType.DMA,
            pltpu.SemaphoreType.DMA((CHUNKS,)),
            pltpu.SemaphoreType.DMA((CHUNKS,)),
            pltpu.SemaphoreType.DMA((CHUNKS,)),
            pltpu.SemaphoreType.DMA((CHUNKS, TAGS)),
            pltpu.SemaphoreType.DMA((CHUNKS, TAGS)),
        ],
        compiler_params=pltpu.CompilerParams(collective_id=0, has_side_effects=True, vmem_limit_bytes=20 * 2**20),
        name="spread",
    )(trainer_gate)
    return pl.pallas_call(
        place,
        out_shape=(
            jax.ShapeDtypeStruct((EXPERTS, CHIPS * SHARE, QB), jnp.bfloat16),
            jax.ShapeDtypeStruct((EXPERTS, CHIPS * BLOCKS, 1), jnp.bfloat16),
        ),
        in_specs=[pl.BlockSpec(memory_space=pltpu.SMEM), pl.BlockSpec(memory_space=pltpu.VMEM)],
        out_specs=(pl.BlockSpec(memory_space=pl.ANY), pl.BlockSpec(memory_space=pltpu.VMEM)),
        scratch_shapes=[pltpu.SemaphoreType.DMA((EXPERTS, CHIPS))],
        compiler_params=pltpu.CompilerParams(vmem_limit_bytes=20 * 2**20),
        name="place",
    )(expert_of_slot, gathered)


def solution(mesh):
    return jax.shard_map(
        shards,
        mesh=mesh,
        in_specs=(P(None, ("rep", "grp"), None), P()),
        out_specs=(P(None, None, "grp"), P(None, None, "grp")),
        check_vma=False,
    )
```

time: 151 us -> 81.1 us (0.54)
  Pallas kernels: 0 us -> 78.2 us
  waiting for transfers between devices: 65.3 us -> 0 us
  blocking collectives: 31.7 us -> 0 us
  local copies, waits for them, and re-layouts: 22 us -> 1.84 us
  other arithmetic: 17.9 us -> 0 us
  between operations: 14.1 us -> 0.66 us
    pallas_call x0 -> x2, Pallas kernels: none -> 78.2 us  [the longest x1 73.2 us: shards(): pl.pallas_call(spread, out_shape=pltpu.VMEM((EXPERTS, CHIPS, FULL, QB), j...]
    all_gather x1 -> x0, waiting for transfers between devices: 65.3 us -> none  [shards(): collected = lax.all_gather(local, 'rep', axis=1, tiled=True)]
    all_to_all x1 -> x0, blocking collectives: 31.7 us -> none  [shards(): lax.all_to_all(placed, 'grp', split_axis=2, concat_axis=1, tiled=True)]
    unnamed x8 -> x4, local copies, waits for them, and re-layouts: 11.9 us -> 1.13 us
    convert_element_type x2 -> x0, other arithmetic: 8.35 us -> none  [the longest x1 7.76 us: quantize(): scaled = (blocks / divisor).astype(jnp.bfloat16).reshape(count, rows, width)]
    reduce_max x2 -> x0, other arithmetic: 8.01 us -> none  [quantize(): largest = jnp.max(jnp.abs(blocks), axis=(2, 4)) + 1e-06]
    all_to_all x2 -> x0, local copies, waits for them, and re-layouts: 5.43 us -> none  [shards(): lax.all_to_all(placed, 'grp', split_axis=2, concat_axis=1, tiled=True)]
    select_n x1 -> x0, local copies, waits for them, and re-layouts: 4.16 us -> none  [shards(): placed = jnp.take(trainer_gate, expert_of_slot, axis=0)]
  transfers between devices with their start and end apart: 1 -> 0, of which waited for: 1 -> 0; matrix products, arithmetic and copies ran while one was open for 0% -> 0% of each run, Pallas kernels for 0% -> 0%
where the time goes in v1:
time: 81.1 us; the launch traced here: 80.7 us
  Pallas kernels  78.2 us (96%)
  local copies, waits for them, and re-layouts  1.84 us (2%)
    pallas_call x1, Pallas kernels, shards(): pl.pallas_call(spread, out_shape=pltpu.VMEM((EXPERTS, CHIPS, FULL, QB), j...  73.2 us
    pallas_call x1, Pallas kernels, shards(): pl.pallas_call(place, out_shape=(jax.ShapeDtypeStruct((EXPERTS, CHIPS * S...  5.02 us

profile of v1, /device:TPU:1, one launch (start us, length us, event | category | flops | bytes accessed | tf_op | source)
XLA Modules:
  0.0 80.7 jit_solution(12539294151188178496)
XLA Ops:
  0.6 0.0 copy-start
  0.6 1.1 %copy-done = bf16[6,28,2048]{2,1,0:T(8,128)(2,1)S(1)} copy-done((bf16[6,28,2048]{2,1,0:T(8,128)(2,1)S(1)}, bf16[6,28,2048]{2,1,0:T(8,128)(2,1)}, u32[]{:S(2)}) %copy-start) | copy-done | bytes 688152
  1.8 0.0 copy-start.1
  1.8 73.2 %spread.1.buf = bf16[6,8,912,128]{3,2,1,0:T(8,128)(2,1)S(1)} custom-call(bf16[6,28,2048]{2,1,0:T(8,128)(2,1)S(1)} %copy-done), custom_call_target="tpu_custom_call" | custom-call | tf_op jit(solution)/shard_map/spread/pallas_call | solution.py:239
  75.0 0.0 copy-done.1
  75.0 5.0 %place.1 = (bf16[6,7168,128]{2,1,0:T(8,128)(2,1)}, bf16[6,56,1]{2,1,0:T(8,128)(2,1)S(1)}) custom-call(s32[6]{0:T(128)S(1)} %copy-done.1, bf16[6,8,912,128]{3,2,1,0:T(8,128)(2,1)S(1)} %spread.1.buf), custom_call_target="tpu_custom_call" | custom-call | tf_op jit(solution)/shard_map/place/pallas_call | solution.py:258
  80.0 0.7 copy.4
Async XLA Ops:
  0.6 1.1 %copy-start = (bf16[6,28,2048]{2,1,0:T(8,128)(2,1)S(1)}, bf16[6,28,2048]{2,1,0:T(8,128)(2,1)}, u32[]{:S(2)}) copy-start(bf16[6,28,2048]{2,1,0:T(8,128)(2,1)} %x_ref.1) | copy-start | bytes 2064388
  1.8 73.2 %copy-start.1 = (s32[6]{0:T(128)S(1)}, s32[6]{0:T(128)}, u32[]{:S(2)}) copy-start(s32[6]{0:T(128)} %slot_ref.1) | copy-start | bytes 76

commit v2 on v1

--- a/solution.py
+++ b/solution.py
@@ -20,11 +20,42 @@
 
 H1 = (0, 448)
 H2 = (448, FULL - 448)
-A1 = (0, 336)
-A2 = (560, FULL - 560)
-B = (336, 224)
+A1 = (0, 288)
+A2 = (608, FULL - 608)
+B = (288, 320)
 ALL = (0, FULL)
 TAGS = 32
+
+STEPS = {
+    "up 1": ((0,), (7,)),
+    "down 2": ((2,), (8,)),
+    "up all": ((1,), (15, 20)),
+    "down all": ((3,), (16, 21)),
+    "side 1": ((4,), (9, 12)),
+    "side 2": ((5,), (11, 10)),
+    "side all": ((6,), (19,)),
+    "far": ((7, 8), (17, 22)),
+    "up side 1": ((9,), (13, 23)),
+    "down side 2": ((11,), (14, 25)),
+    "up side 2": ((10,), (24,)),
+    "down side 1": ((12,), (26,)),
+    "up between": ((15,), (29,)),
+    "down between": ((16,), (30,)),
+    "far between": ((17,), (31,)),
+    "far side 1": ((13,), (27,)),
+    "far side 2": ((14,), (28,)),
+}
+ORDER = (
+    ("scale", 0), ("up 1", 0), ("down 2", 0), ("scale", 1), ("up all", 0), ("down all", 0), ("side 1", 0), ("far", 0),
+    ("scale", 2), ("side 2", 0), ("up 1", 1), ("down 2", 1), ("side all", 0), ("side 1", 1), ("up all", 1),
+    ("down all", 1), ("side 2", 1), ("up side 1", 0), ("down side 1", 0), ("side all", 1), ("up 1", 2), ("down 2", 2),
+    ("up between", 0), ("down between", 0), ("up all", 2), ("down all", 2), ("far between", 0), ("up side 2", 0),
+    ("down side 2", 0), ("side 1", 2), ("far", 1), ("side 2", 2), ("up side 1", 1), ("down side 1", 1), ("side all", 2),
+    ("up side 2", 1), ("down side 2", 1), ("up between", 1), ("far side 1", 0), ("down between", 1), ("far", 2),
+    ("far side 2", 0), ("up between", 2), ("up side 1", 2), ("down side 1", 2), ("down between", 2), ("up side 2", 2),
+    ("down side 2", 2), ("far between", 1), ("far side 1", 1), ("far side 2", 1), ("far between", 2),
+    ("far side 1", 2), ("far side 2", 2),
+)
 
 
 def spread(x_ref, buf, xv, got, rows, load_sem, own_sem, out_sem, in_sem, ssem, rsem):
@@ -162,53 +193,12 @@
         buf[e, here, pl.ds(SHARE, 16), :] = scales.astype(jnp.bfloat16)
         send(k, 0, 2, 4, 5, 1, 3, 6, 18)
 
-    def early(k):
-        wait(k, 0)
-        send(k, 7)
-        wait(k, 2)
-        send(k, 8)
-        wait(k, 4)
-        send(k, 9, 12)
-        wait(k, 5)
-        send(k, 11, 10)
-        wait(k, 1)
-        send(k, 15, 20)
-        wait(k, 3)
-        send(k, 16, 21)
-        wait(k, 6)
-        send(k, 19)
-        wait(k, 7, 8)
-        send(k, 17, 22)
-
-    def late(k):
-        wait(k, 9)
-        send(k, 13, 23)
-        wait(k, 11)
-        send(k, 14, 25)
-        wait(k, 10)
-        send(k, 24)
-        wait(k, 12)
-        send(k, 26)
-        wait(k, 15)
-        send(k, 29)
-        wait(k, 16)
-        send(k, 30)
-        wait(k, 13)
-        send(k, 27)
-        wait(k, 14)
-        send(k, 28)
-        wait(k, 17)
-        send(k, 31)
-
-    scale(0)
-    early(0)
-    scale(1)
-    late(0)
-    early(1)
-    scale(2)
-    late(1)
-    early(2)
-    late(2)
+    for step, k in ORDER:
+        if step == "scale":
+            scale(k)
+        else:
+            wait(k, *STEPS[step][0])
+            send(k, *STEPS[step][1])
     for k in range(CHUNKS):
         for t in range(18, TAGS):
             wait(k, t)
@@ -217,22 +207,33 @@
         pltpu.make_async_copy(got.at[k, pl.ds(0, SOURCES - 1)], got.at[k, pl.ds(0, SOURCES - 1)], out_sem.at[k]).wait()
 
 
-def place(slot_ref, buf, out_ref, scale_ref, sem):
+def place(slot_ref, buf, out_ref, scale_ref, found, sem, scale_sem):
     for s in range(EXPERTS):
         e = slot_ref[s]
         for ch in range(CHIPS):
             pltpu.make_async_copy(
                 buf.at[e, ch, pl.ds(0, SHARE)], out_ref.at[s, pl.ds(ch * SHARE, SHARE)], sem.at[s, ch]
             ).start()
+    row = lax.broadcasted_iota(jnp.int32, (16, QB), 0)
+    lane = lax.broadcasted_iota(jnp.int32, (16, QB), 1)
+    lines = jnp.zeros((16, QB), jnp.float32)
     for s in range(EXPERTS):
         e = slot_ref[s]
-        parts = [buf[e, ch, pl.ds(SHARE, 16), :].astype(jnp.float32)[:BLOCKS] for ch in range(CHIPS)]
-        scale_ref[s] = jnp.concatenate(parts, axis=0)[:, 0:1].astype(jnp.bfloat16)
+        line = jnp.zeros((16, QB), jnp.float32)
+        for ch in range(CHIPS):
+            here = (lane - row == ch * BLOCKS) & (row < BLOCKS)
+            line += jnp.where(here, buf[e, ch, pl.ds(SHARE, 16), :].astype(jnp.float32), 0.0)
+        line = jnp.sum(line, axis=0, keepdims=True)
+        lines = jnp.where(row == s, jnp.broadcast_to(line, (16, QB)), lines)
+    found[...] = lines[:EXPERTS, : CHIPS * BLOCKS].astype(jnp.bfloat16)
+    out = pltpu.make_async_copy(found, scale_ref, scale_sem)
+    out.start()
     for s in range(EXPERTS):
         for ch in range(CHIPS):
             pltpu.make_async_copy(
                 buf.at[0, ch, pl.ds(0, SHARE)], out_ref.at[s, pl.ds(ch * SHARE, SHARE)], sem.at[s, ch]
             ).wait()
+    out.wait()
 
 
 def shards(trainer_gate, expert_of_slot):
@@ -252,21 +253,26 @@
             pltpu.SemaphoreType.DMA((CHUNKS, TAGS)),
             pltpu.SemaphoreType.DMA((CHUNKS, TAGS)),
         ],
-        compiler_params=pltpu.CompilerParams(collective_id=0, has_side_effects=True, vmem_limit_bytes=20 * 2**20),
+        compiler_params=pltpu.CompilerParams(collective_id=0, has_side_effects=True, vmem_limit_bytes=52 * 2**20),
         name="spread",
     )(trainer_gate)
-    return pl.pallas_call(
+    placed, scales = pl.pallas_call(
         place,
         out_shape=(
             jax.ShapeDtypeStruct((EXPERTS, CHIPS * SHARE, QB), jnp.bfloat16),
-            jax.ShapeDtypeStruct((EXPERTS, CHIPS * BLOCKS, 1), jnp.bfloat16),
+            jax.ShapeDtypeStruct((EXPERTS, CHIPS * BLOCKS), jnp.bfloat16),
         ),
         in_specs=[pl.BlockSpec(memory_space=pltpu.SMEM), pl.BlockSpec(memory_space=pltpu.VMEM)],
-        out_specs=(pl.BlockSpec(memory_space=pl.ANY), pl.BlockSpec(memory_space=pltpu.VMEM)),
-        scratch_shapes=[pltpu.SemaphoreType.DMA((EXPERTS, CHIPS))],
+        out_specs=(pl.BlockSpec(memory_space=pl.ANY), pl.BlockSpec(memory_space=pl.ANY)),
+        scratch_shapes=[
+            pltpu.VMEM((EXPERTS, CHIPS * BLOCKS), jnp.bfloat16),
+            pltpu.SemaphoreType.DMA((EXPERTS, CHIPS)),
+            pltpu.SemaphoreType.DMA,
+        ],
         compiler_params=pltpu.CompilerParams(vmem_limit_bytes=20 * 2**20),
         name="place",
     )(expert_of_slot, gathered)
+    return placed, scales.reshape(EXPERTS, CHIPS * BLOCKS, 1)
 
 
 def solution(mesh):

time: 81.1 us -> 70.5 us (0.87)
  Pallas kernels: 78.2 us -> 69.7 us
  local copies, waits for them, and re-layouts: 1.84 us -> 0.01 us
    pallas_call x1, Pallas kernels: 73.2 us -> 64.7 us  [shards(): pl.pallas_call(spread, out_shape=pltpu.VMEM((EXPERTS, CHIPS, FULL, QB), j...]
    unnamed x4 -> x2, local copies, waits for them, and re-layouts: 1.13 us -> 0.01 us
where the time goes in v2:
time: 70.5 us; the launch traced here: 70.4 us
  Pallas kernels  69.7 us (99%)
    pallas_call x1, Pallas kernels, shards(): pl.pallas_call(spread, out_shape=pltpu.VMEM((EXPERTS, CHIPS, FULL, QB), j...  64.7 us
    pallas_call x1, Pallas kernels, shards(): pl.pallas_call(place, out_shape=(jax.ShapeDtypeStruct((EXPERTS, CHIPS * S...  5.03 us

profile of v2, /device:TPU:1, one launch (start us, length us, event | category | flops | bytes accessed | tf_op | source)
XLA Modules:
  0.0 70.4 jit_solution(5040451240172250303)
XLA Ops:
  0.6 0.0 copy-start
  0.6 64.7 %spread.1.buf = bf16[6,8,912,128]{3,2,1,0:T(8,128)(2,1)S(1)} custom-call(bf16[6,28,2048]{2,1,0:T(8,128)(2,1)} %x_ref.1), custom_call_target="tpu_custom_call" | custom-call | tf_op jit(solution)/shard_map/spread/pallas_call | solution.py:240
  65.4 0.0 copy-done
  65.4 5.0 %place.1 = (bf16[6,7168,128]{2,1,0:T(8,128)(2,1)}, bf16[6,56]{1,0:T(8,128)(2,1)}) custom-call(s32[6]{0:T(128)S(1)} %copy-done, bf16[6,8,912,128]{3,2,1,0:T(8,128)(2,1)S(1)} %spread.1.buf), custom_call_target="tpu_custom_call" | custom-call | tf_op jit(solution)/shard_map/place/pallas_call | solution.py:259
Async XLA Ops:
  0.6 64.7 %copy-start = (s32[6]{0:T(128)S(1)}, s32[6]{0:T(128)}, u32[]{:S(2)}) copy-start(s32[6]{0:T(128)} %slot_ref.1) | copy-start | bytes 76

commit v3 on v2

v3 whole, which is shorter than its diff:
```python
import jax
import jax.numpy as jnp
from jax import lax
from jax.experimental import pallas as pl
from jax.experimental.pallas import tpu as pltpu
from jax.sharding import PartitionSpec as P

MESH = pl.DeviceIdType.MESH
EXPERTS, ROWS, FF = 6, 28, 2048
QB = 128
NX, NZ, NY, CORES = 4, 4, 4, 2
SHARE = 32 * ROWS
BLOCKS = SHARE // QB
CHIPS = 8
BATCHES = ((0, 4), (4, 2))
PIECE = (112, 64)

SAME, NEAR, AWAY = range(3)
CHUNKS = ((0, SAME), (0, NEAR), (0, AWAY), (1, SAME), (1, NEAR), (1, AWAY))
SOURCES = {SAME: 4, NEAR: 8, AWAY: 4}
ENDS = (208, 288, 112, 96, 144, 64)
TAGS = 32
H1, H2, A1, A2, MID, ALL = range(6)

(
    UP_1, DOWN_2, UP_ALL, DOWN_ALL, SIDE_1, SIDE_2,
    SIDE_ALL, FAR, UP_SIDE_1, DOWN_SIDE_2, UP_SIDE_2, DOWN_SIDE_1,
    UP_BETWEEN, DOWN_BETWEEN, FAR_BETWEEN, FAR_SIDE_1, FAR_SIDE_2,
) = range(17)
OWN, SCALE, ROUND = range(17, 20)
STEPS = {
    UP_1: ((0,), (7,)),
    DOWN_2: ((2,), (8,)),
    UP_ALL: ((1,), (15, 20)),
    DOWN_ALL: ((3,), (16, 21)),
    SIDE_1: ((4,), (9, 12)),
    SIDE_2: ((5,), (11, 10)),
    SIDE_ALL: ((6,), (19,)),
    FAR: ((7, 8), (17, 22)),
    UP_SIDE_1: ((9,), (13, 23)),
    DOWN_SIDE_2: ((11,), (14, 25)),
    UP_SIDE_2: ((10,), (24,)),
    DOWN_SIDE_1: ((12,), (26,)),
    UP_BETWEEN: ((15,), (29,)),
    DOWN_BETWEEN: ((16,), (30,)),
    FAR_BETWEEN: ((17,), (31,)),
    FAR_SIDE_1: ((13,), (27,)),
    FAR_SIDE_2: ((14,), (28,)),
}
FROM_TWIN = ((18, 19), (21, 25, 26, 30), (22, 27, 28, 31), (20, 23, 24, 29))
ORDER = (
    (ROUND, 0), (OWN, 0), (OWN, 3), (ROUND, 1), (ROUND, 2), (UP_1, 0), (DOWN_2, 0), (SIDE_1, 0), (UP_ALL, 0),
    (SIDE_2, 0), (DOWN_ALL, 0), (SIDE_ALL, 0), (UP_1, 3), (SIDE_1, 3), (DOWN_2, 3), (SIDE_2, 3), (UP_ALL, 3),
    (DOWN_ALL, 3), (SIDE_ALL, 3), (FAR, 0), (UP_SIDE_1, 0), (DOWN_SIDE_1, 0), (OWN, 1), (UP_SIDE_2, 0),
    (DOWN_SIDE_2, 0), (DOWN_SIDE_1, 3), (UP_SIDE_1, 3), (FAR, 3), (UP_SIDE_2, 3), (DOWN_SIDE_2, 3), (FAR_SIDE_1, 0),
    (UP_BETWEEN, 0), (DOWN_BETWEEN, 0), (UP_BETWEEN, 3), (OWN, 2), (DOWN_BETWEEN, 3), (DOWN_2, 1), (FAR_BETWEEN, 0),
    (UP_1, 1), (OWN, 4), (SIDE_1, 1), (DOWN_ALL, 1), (SIDE_2, 1), (UP_ALL, 1), (FAR_SIDE_2, 0), (FAR_SIDE_1, 3),
    (FAR_SIDE_2, 3), (SIDE_ALL, 1), (UP_1, 2), (DOWN_2, 2), (OWN, 5), (FAR_BETWEEN, 3), (SIDE_1, 2), (UP_ALL, 2),
    (DOWN_ALL, 2), (SIDE_2, 2), (SIDE_ALL, 2), (SIDE_1, 4), (FAR, 1), (SCALE, 0), (SIDE_2, 4), (UP_1, 4), (DOWN_2, 4),
    (SCALE, 1), (SIDE_ALL, 4), (UP_ALL, 4), (DOWN_ALL, 4), (DOWN_BETWEEN, 1), (UP_SIDE_1, 1), (DOWN_SIDE_1, 1),
    (UP_BETWEEN, 1), (SIDE_1, 5), (SIDE_2, 5), (UP_SIDE_2, 1), (DOWN_SIDE_2, 1), (SIDE_ALL, 5), (FAR, 2),
    (UP_BETWEEN, 2), (SCALE, 8), (UP_1, 5), (DOWN_2, 5), (SCALE, 9), (UP_ALL, 5), (DOWN_ALL, 5), (DOWN_BETWEEN, 2),
    (UP_SIDE_1, 2), (DOWN_SIDE_1, 2), (UP_SIDE_2, 2), (DOWN_SIDE_2, 2), (UP_SIDE_1, 4), (DOWN_SIDE_1, 4),
    (FAR_BETWEEN, 1), (SCALE, 6), (UP_SIDE_2, 4), (DOWN_SIDE_2, 4), (UP_BETWEEN, 4), (SCALE, 7), (FAR, 4),
    (DOWN_SIDE_1, 5), (DOWN_BETWEEN, 4), (DOWN_SIDE_2, 5), (SCALE, 2), (FAR_SIDE_1, 1), (FAR_BETWEEN, 2),
    (UP_SIDE_1, 5), (UP_SIDE_2, 5), (FAR_SIDE_2, 1), (UP_BETWEEN, 5), (SCALE, 3), (FAR, 5), (DOWN_BETWEEN, 5),
    (FAR_SIDE_1, 2), (SCALE, 14), (FAR_SIDE_2, 2), (SCALE, 15), (FAR_BETWEEN, 4), (FAR_SIDE_1, 4), (FAR_SIDE_2, 4),
    (FAR_SIDE_1, 5), (FAR_SIDE_2, 5), (SCALE, 10), (SCALE, 11), (FAR_BETWEEN, 5), (SCALE, 4), (SCALE, 5), (SCALE, 12),
    (SCALE, 13),
)


def spread(
    x_ref, buf, xv, stage0, stage1, raw0, raw1, rows, load_sem, own_sem, out_sem, in_sem, ready, ssem, rsem
):
    g, r = lax.axis_index("grp"), lax.axis_index("rep")
    x, zh = g // NZ, g % NZ
    y, z, c = r // 4, (r // 2) % 2, r % 2
    stage, raw = (stage0, stage1), (raw0, raw1)

    load = pltpu.make_async_copy(x_ref, xv, load_sem)
    load.start()

    def at(gx, gz, yy, zz, cc):
        return (gx % NX * NZ + gz % NZ, (yy % NY * 2 + zz) * 2 + cc)

    up, down = at(x, zh, y + 1, z, c), at(x, zh, y + 3, z, c)
    side, twin = at(x, zh, y, 1 - z, c), at(x, zh, y, z, 1 - c)
    out = at(x, zh + 3 + 2 * z, y, 1 - z, c)
    line = [at(x + d, zh, y, z, c) for d in (2, 1, 3)]
    near = line + [out, up, down, side, twin]

    def signal(sem, devices):
        for d in devices:
            pl.semaphore_signal(sem, inc=1, device_id=d, device_id_type=MESH)

    barrier = pltpu.get_barrier_semaphore()
    signal(barrier, near)

    load.wait()

    def pack(i, carry):
        col = pl.ds(pl.multiple_of(i * QB, QB), QB)
        for b, (first, count) in enumerate(BATCHES):
            for e in range(count):
                rows[0, pl.ds(e * ROWS, ROWS), :] = xv[first + e, :, col].astype(jnp.float32)
            stage[b][i] = rows[0, pl.ds(0, PIECE[b]), :].astype(jnp.bfloat16)
        return carry

    lax.fori_loop(0, NX * NZ, pack, 0)
    here = [pl.ds(pl.multiple_of((z * 4 + x) * n, 16), n) for n in PIECE]
    for b in range(2):
        pltpu.make_async_copy(stage[b].at[g], raw[b].at[y, c, zh, here[b]], own_sem.at[b]).start()

    def give(b, kind, gz, zz, dxs):
        for dx in dxs:
            pltpu.make_async_remote_copy(
                src_ref=stage[b].at[(x + dx) % NX * NZ + gz % NZ],
                dst_ref=raw[b].at[y, c, zh, here[b]],
                send_sem=out_sem.at[b, kind],
                recv_sem=in_sem.at[b, kind],
                device_id=at(x + dx, gz, y, zz, c),
                device_id_type=MESH,
            ).start()

    def region(k, chip):
        b, kind = CHUNKS[k]
        n = SOURCES[kind] * PIECE[b]
        if kind == SAME:
            return zh, chip[1] * n, n
        if kind == NEAR:
            return (zh + 3 + 2 * chip[1]) % NZ, 0, n
        return (zh + 2) % NZ, (1 - chip[1]) * n, n

    def part(k, chip, core, first, n):
        gz, base, _ = region(k, chip)
        return raw[CHUNKS[k][0]].at[chip[0], core, gz, pl.ds(pl.multiple_of(base + first, 16), n)]

    def chip(dy, dz):
        return ((y + dy) % NY, (z + dz) % 2)

    def pieces(k):
        n = SOURCES[CHUNKS[k][1]] * PIECE[CHUNKS[k][0]]
        a, h = ENDS[k], n // 2
        return {H1: (0, h), H2: (h, h), A1: (0, a), A2: (n - a, a), MID: (a, n - 2 * a), ALL: (0, n)}

    plan = {
        0: (chip(0, 0), H1, up),
        1: (chip(0, 0), H2, up),
        2: (chip(0, 0), H2, down),
        3: (chip(0, 0), H1, down),
        4: (chip(0, 0), A1, side),
        5: (chip(0, 0), A2, side),
        6: (chip(0, 0), MID, side),
        7: (chip(3, 0), H1, up),
        8: (chip(1, 0), H2, down),
        9: (chip(0, 1), A1, up),
        10: (chip(0, 1), A2, up),
        11: (chip(0, 1), A2, down),
        12: (chip(0, 1), A1, down),
        13: (chip(3, 1), A1, up),
        14: (chip(1, 1), A2, down),
        15: (chip(3, 0), MID, side),
        16: (chip(1, 0), MID, side),
        17: (chip(2, 0), MID, side),
        18: (chip(0, 0), ALL, twin),
        19: (chip(0, 1), ALL, twin),
        20: (chip(3, 0), ALL, twin),
        21: (chip(1, 0), ALL, twin),
        22: (chip(2, 0), ALL, twin),
        23: (chip(3, 1), A1, twin),
        24: (chip(3, 1), A2, twin),
        25: (chip(1, 1), A2, twin),
        26: (chip(1, 1), A1, twin),
        27: (chip(2, 1), A1, twin),
        28: (chip(2, 1), A2, twin),
        29: (chip(3, 1), MID, twin),
        30: (chip(1, 1), MID, twin),
        31: (chip(2, 1), MID, twin),
    }
    came = {
        0: chip(3, 0), 1: chip(3, 0), 2: chip(1, 0), 3: chip(1, 0),
        4: chip(0, 1), 5: chip(0, 1), 6: chip(0, 1),
        7: chip(2, 0), 8: chip(2, 0),
        9: chip(3, 1), 10: chip(3, 1), 11: chip(1, 1), 12: chip(1, 1),
        13: chip(2, 1), 14: chip(2, 1),
        15: chip(3, 1), 16: chip(1, 1), 17: chip(2, 1),
    }

    def copy(k, tag, origin, core):
        _, piece, target = plan[tag]
        ref = part(k, origin, core, *pieces(k)[piece])
        return pltpu.make_async_remote_copy(
            src_ref=ref,
            dst_ref=ref,
            send_sem=ssem.at[k, tag],
            recv_sem=rsem.at[k, tag],
            device_id=target,
            device_id_type=MESH,
        )

    def send(k, *tags):
        for t in tags:
            copy(k, t, plan[t][0], c).start()

    def wait(k, *tags):
        for t in tags:
            copy(k, t, came[t] if t < 18 else plan[t][0], c if t < 18 else 1 - c).wait_recv()

    def own(k):
        b, kind = CHUNKS[k]
        lot = 3 if kind == SAME else SOURCES[kind]
        if kind == SAME:
            pltpu.make_async_copy(stage[b].at[g], raw[b].at[y, c, zh, here[b]], own_sem.at[b]).wait()
        got = part(k, chip(0, 0), c, 0, lot * PIECE[b])
        pltpu.make_async_copy(got, got, in_sem.at[b, k % 3]).wait()
        send(k, 0, 2, 4, 5, 1, 3, 6, 18)

    def scale(b, dy, zs):
        if zs == 0:
            for k in range(3 * b, 3 * b + 3):
                wait(k, *FROM_TWIN[dy])
        first, count = BATCHES[b]
        n, ys = PIECE[b], (y + dy) % NY

        def fetch(i, carry):
            cc, xs = i // NX, i % NX
            at_row = pl.ds(pl.multiple_of((zs * 4 + xs) * n, 16), n)
            to = rows.at[:, pl.ds(pl.multiple_of(i * 4 * ROWS, 16), 4 * ROWS), :]
            for gz in range(NZ):
                v = raw[b][ys, cc, gz, at_row, :].astype(jnp.float32)
                for e in range(count):
                    to[e, pl.ds(gz * ROWS, ROWS), :] = v[e * ROWS : (e + 1) * ROWS]
            return carry

        lax.fori_loop(0, CORES * NX, fetch, 0)
        row = lax.broadcasted_iota(jnp.int32, (16, QB), 0)

        def expert(e, carry):
            found = jnp.zeros((16, QB), jnp.float32)
            for blk in range(BLOCKS):
                v = rows[e, pl.ds(blk * QB, QB), :]
                m = jnp.max(jnp.max(jnp.abs(v), axis=0, keepdims=True), axis=1, keepdims=True) + 1e-06
                s = jnp.broadcast_to(m, (16, QB)).astype(jnp.bfloat16).astype(jnp.float32)
                buf[first + e, ys * 2 + zs, pl.ds(blk * QB, QB), :] = (v / s[0:1]).astype(jnp.bfloat16)
                found = jnp.where(row == blk, s, found)
            buf[first + e, ys * 2 + zs, pl.ds(SHARE, 16), :] = found.astype(jnp.bfloat16)
            return carry

        lax.fori_loop(0, count, expert, 0)

    def further(i):
        pl.semaphore_wait(ready.at[i], len(line) + 2 if i == 0 else 2)
        if i < 2:
            signal(ready.at[i + 1], [side, out])
        if i == 0:
            give(0, NEAR, zh + 3 + 2 * z, 1 - z, (2, 1, 3, 0))
        elif i == 1:
            give(0, NEAR, zh + 1 + 2 * z, z, (2, 1, 3, 0))
        else:
            give(0, AWAY, zh + 2, 1 - z, (2, 1, 3, 0))
            give(1, NEAR, zh + 3 + 2 * z, 1 - z, (2, 1, 3, 0))
            give(1, NEAR, zh + 1 + 2 * z, z, (2, 1, 3, 0))
            give(1, AWAY, zh + 2, 1 - z, (2, 1, 3, 0))

    pl.semaphore_wait(barrier, len(near))
    signal(ready.at[0], line + [side, out])
    for b in range(2):
        give(b, SAME, zh, z, (2, 1, 3))

    for step, k in ORDER:
        if step == ROUND:
            further(k)
        elif step == OWN:
            own(k)
        elif step == SCALE:
            scale(k // 8, k // 2 % NY, k % 2)
        else:
            wait(k, *STEPS[step][0])
            send(k, *STEPS[step][1])

    for k, (b, kind) in enumerate(CHUNKS):
        for t in range(TAGS):
            copy(k, t, plan[t][0], c).wait_send()
        lot = 3 if kind == SAME else SOURCES[kind]
        gone = part(k, chip(0, 0), c, 0, lot * PIECE[b])
        pltpu.make_async_copy(gone, gone, out_sem.at[b, k % 3]).wait()


def place(slot_ref, buf, out_ref, scale_ref, found, sem, scale_sem):
    for s in range(EXPERTS):
        e = slot_ref[s]
        for ch in range(CHIPS):
            pltpu.make_async_copy(
                buf.at[e, ch, pl.ds(0, SHARE)], out_ref.at[s, pl.ds(ch * SHARE, SHARE)], sem.at[s, ch]
            ).start()
    row = lax.broadcasted_iota(jnp.int32, (16, QB), 0)
    lane = lax.broadcasted_iota(jnp.int32, (16, QB), 1)
    lines = jnp.zeros((16, QB), jnp.float32)
    for s in range(EXPERTS):
        e = slot_ref[s]
        line = jnp.zeros((16, QB), jnp.float32)
        for ch in range(CHIPS):
            here = (lane - row == ch * BLOCKS) & (row < BLOCKS)
            line += jnp.where(here, buf[e, ch, pl.ds(SHARE, 16), :].astype(jnp.float32), 0.0)
        line = jnp.sum(line, axis=0, keepdims=True)
        lines = jnp.where(row == s, jnp.broadcast_to(line, (16, QB)), lines)
    found[...] = lines[:EXPERTS, : CHIPS * BLOCKS].astype(jnp.bfloat16)
    out = pltpu.make_async_copy(found, scale_ref, scale_sem)
    out.start()
    for s in range(EXPERTS):
        for ch in range(CHIPS):
            pltpu.make_async_copy(
                buf.at[0, ch, pl.ds(0, SHARE)], out_ref.at[s, pl.ds(ch * SHARE, SHARE)], sem.at[s, ch]
            ).wait()
    out.wait()


def shards(trainer_gate, expert_of_slot):
    rest = [pltpu.VMEM((NY, CORES, NZ, 8 * n, QB), jnp.bfloat16) for n in PIECE]
    ready_to_go = [pltpu.VMEM((NX * NZ, n, QB), jnp.bfloat16) for n in PIECE]
    gathered = pl.pallas_call(
        spread,
        out_shape=pltpu.VMEM((EXPERTS, CHIPS, SHARE + 16, QB), jnp.bfloat16),
        in_specs=[pl.BlockSpec(memory_space=pl.ANY)],
        out_specs=pl.BlockSpec(memory_space=pltpu.VMEM),
        scratch_shapes=[
            pltpu.VMEM((EXPERTS, ROWS, FF), jnp.bfloat16),
            *ready_to_go,
            *rest,
            pltpu.VMEM((4, SHARE, QB), jnp.float32),
            pltpu.SemaphoreType.DMA,
            pltpu.SemaphoreType.DMA((2,)),
            pltpu.SemaphoreType.DMA((2, 3)),
            pltpu.SemaphoreType.DMA((2, 3)),
            pltpu.SemaphoreType.REGULAR((3,)),
            pltpu.SemaphoreType.DMA((len(CHUNKS), TAGS)),
            pltpu.SemaphoreType.DMA((len(CHUNKS), TAGS)),
        ],
        compiler_params=pltpu.CompilerParams(collective_id=0, has_side_effects=True, vmem_limit_bytes=52 * 2**20),
        name="spread",
    )(trainer_gate)
    placed, scales = pl.pallas_call(
        place,
        out_shape=(
            jax.ShapeDtypeStruct((EXPERTS, CHIPS * SHARE, QB), jnp.bfloat16),
            jax.ShapeDtypeStruct((EXPERTS, CHIPS * BLOCKS), jnp.bfloat16),
        ),
        in_specs=[
            pl.BlockSpec(memory_space=pltpu.SMEM),
            pl.BlockSpec(memory_space=pltpu.VMEM),
        ],
        out_specs=(pl.BlockSpec(memory_space=pl.ANY), pl.BlockSpec(memory_space=pl.ANY)),
        scratch_shapes=[
            pltpu.VMEM((EXPERTS, CHIPS * BLOCKS), jnp.bfloat16),
            pltpu.SemaphoreType.DMA((EXPERTS, CHIPS)),
            pltpu.SemaphoreType.DMA,
        ],
        compiler_params=pltpu.CompilerParams(vmem_limit_bytes=20 * 2**20),
        name="place",
    )(expert_of_slot, gathered)
    return placed, scales.reshape(EXPERTS, CHIPS * BLOCKS, 1)


def solution(mesh):
    return jax.shard_map(
        shards,
        mesh=mesh,
        in_specs=(P(None, ("rep", "grp"), None), P()),
        out_specs=(P(None, None, "grp"), P(None, None, "grp")),
        check_vma=False,
    )
```

time: 70.5 us -> 66.9 us (0.949)
  Pallas kernels: 69.7 us -> 66.2 us
    pallas_call x1, Pallas kernels: 64.7 us -> 61.2 us  [shards(): pl.pallas_call(spread, out_shape=pltpu.VMEM((EXPERTS, CHIPS, SHARE + 16,...]
where the time goes in v3:
time: 66.9 us; the launch traced here: 66.8 us
  Pallas kernels  66.2 us (99%)
    pallas_call x1, Pallas kernels, shards(): pl.pallas_call(spread, out_shape=pltpu.VMEM((EXPERTS, CHIPS, SHARE + 16,...  61.2 us
    pallas_call x1, Pallas kernels, shards(): pl.pallas_call(place, out_shape=(jax.ShapeDtypeStruct((EXPERTS, CHIPS * S...  5.03 us

profile of v3, /device:TPU:1, one launch (start us, length us, event | category | flops | bytes accessed | tf_op | source)
XLA Modules:
  0.0 66.8 jit_solution(1385290018419808161)
XLA Ops:
  0.6 0.0 copy-start
  0.6 61.2 %spread.1.buf = bf16[6,8,912,128]{3,2,1,0:T(8,128)(2,1)S(1)} custom-call(bf16[6,28,2048]{2,1,0:T(8,128)(2,1)} %x_ref.1), custom_call_target="tpu_custom_call" | custom-call | tf_op jit(solution)/shard_map/spread/pallas_call | solution.py:322
  61.8 0.0 copy-done
  61.8 5.0 %place.1 = (bf16[6,7168,128]{2,1,0:T(8,128)(2,1)}, bf16[6,56]{1,0:T(8,128)(2,1)}) custom-call(s32[6]{0:T(128)S(1)} %copy-done, bf16[6,8,912,128]{3,2,1,0:T(8,128)(2,1)S(1)} %spread.1.buf), custom_call_target="tpu_custom_call" | custom-call | tf_op jit(solution)/shard_map/place/pallas_call | solution.py:343
Async XLA Ops:
  0.6 61.2 %copy-start = (s32[6]{0:T(128)S(1)}, s32[6]{0:T(128)}, u32[]{:S(2)}) copy-start(s32[6]{0:T(128)} %slot_ref.1) | copy-start | bytes 76

commit v4 on v3

--- a/solution.py
+++ b/solution.py
@@ -18,7 +18,7 @@
 SAME, NEAR, AWAY = range(3)
 CHUNKS = ((0, SAME), (0, NEAR), (0, AWAY), (1, SAME), (1, NEAR), (1, AWAY))
 SOURCES = {SAME: 4, NEAR: 8, AWAY: 4}
-ENDS = (208, 288, 112, 96, 144, 64)
+ENDS = (208, 256, 128, 112, 112, 80)
 TAGS = 32
 H1, H2, A1, A2, MID, ALL = range(6)
 
@@ -48,25 +48,31 @@
     FAR_SIDE_2: ((14,), (28,)),
 }
 FROM_TWIN = ((18, 19), (21, 25, 26, 30), (22, 27, 28, 31), (20, 23, 24, 29))
+WHOLE = (0, 1, 2, 3, 4, )
+WHOLE_STEPS = {
+    **STEPS,
+    UP_SIDE_1: ((9,), (13,)),
+    DOWN_SIDE_2: ((11,), (14,)),
+    UP_SIDE_2: ((10, 15), (23,)),
+    DOWN_SIDE_1: ((12, 16), (25,)),
+    FAR_SIDE_1: ((13, 14, 17), (27,)),
+}
+WHOLE_FROM_TWIN = ((18, 19), (21, 25), (22, 27), (20, 23))
 ORDER = (
     (ROUND, 0), (OWN, 0), (OWN, 3), (ROUND, 1), (ROUND, 2), (UP_1, 0), (DOWN_2, 0), (SIDE_1, 0), (UP_ALL, 0),
-    (SIDE_2, 0), (DOWN_ALL, 0), (SIDE_ALL, 0), (UP_1, 3), (SIDE_1, 3), (DOWN_2, 3), (SIDE_2, 3), (UP_ALL, 3),
-    (DOWN_ALL, 3), (SIDE_ALL, 3), (FAR, 0), (UP_SIDE_1, 0), (DOWN_SIDE_1, 0), (OWN, 1), (UP_SIDE_2, 0),
-    (DOWN_SIDE_2, 0), (DOWN_SIDE_1, 3), (UP_SIDE_1, 3), (FAR, 3), (UP_SIDE_2, 3), (DOWN_SIDE_2, 3), (FAR_SIDE_1, 0),
-    (UP_BETWEEN, 0), (DOWN_BETWEEN, 0), (UP_BETWEEN, 3), (OWN, 2), (DOWN_BETWEEN, 3), (DOWN_2, 1), (FAR_BETWEEN, 0),
-    (UP_1, 1), (OWN, 4), (SIDE_1, 1), (DOWN_ALL, 1), (SIDE_2, 1), (UP_ALL, 1), (FAR_SIDE_2, 0), (FAR_SIDE_1, 3),
-    (FAR_SIDE_2, 3), (SIDE_ALL, 1), (UP_1, 2), (DOWN_2, 2), (OWN, 5), (FAR_BETWEEN, 3), (SIDE_1, 2), (UP_ALL, 2),
-    (DOWN_ALL, 2), (SIDE_2, 2), (SIDE_ALL, 2), (SIDE_1, 4), (FAR, 1), (SCALE, 0), (SIDE_2, 4), (UP_1, 4), (DOWN_2, 4),
-    (SCALE, 1), (SIDE_ALL, 4), (UP_ALL, 4), (DOWN_ALL, 4), (DOWN_BETWEEN, 1), (UP_SIDE_1, 1), (DOWN_SIDE_1, 1),
-    (UP_BETWEEN, 1), (SIDE_1, 5), (SIDE_2, 5), (UP_SIDE_2, 1), (DOWN_SIDE_2, 1), (SIDE_ALL, 5), (FAR, 2),
-    (UP_BETWEEN, 2), (SCALE, 8), (UP_1, 5), (DOWN_2, 5), (SCALE, 9), (UP_ALL, 5), (DOWN_ALL, 5), (DOWN_BETWEEN, 2),
-    (UP_SIDE_1, 2), (DOWN_SIDE_1, 2), (UP_SIDE_2, 2), (DOWN_SIDE_2, 2), (UP_SIDE_1, 4), (DOWN_SIDE_1, 4),
-    (FAR_BETWEEN, 1), (SCALE, 6), (UP_SIDE_2, 4), (DOWN_SIDE_2, 4), (UP_BETWEEN, 4), (SCALE, 7), (FAR, 4),
-    (DOWN_SIDE_1, 5), (DOWN_BETWEEN, 4), (DOWN_SIDE_2, 5), (SCALE, 2), (FAR_SIDE_1, 1), (FAR_BETWEEN, 2),
-    (UP_SIDE_1, 5), (UP_SIDE_2, 5), (FAR_SIDE_2, 1), (UP_BETWEEN, 5), (SCALE, 3), (FAR, 5), (DOWN_BETWEEN, 5),
-    (FAR_SIDE_1, 2), (SCALE, 14), (FAR_SIDE_2, 2), (SCALE, 15), (FAR_BETWEEN, 4), (FAR_SIDE_1, 4), (FAR_SIDE_2, 4),
-    (FAR_SIDE_1, 5), (FAR_SIDE_2, 5), (SCALE, 10), (SCALE, 11), (FAR_BETWEEN, 5), (SCALE, 4), (SCALE, 5), (SCALE, 12),
-    (SCALE, 13),
+    (SIDE_2, 0), (DOWN_ALL, 0), (SIDE_ALL, 0), (UP_1, 3), (DOWN_2, 3), (SIDE_1, 3), (UP_ALL, 3), (SIDE_2, 3),
+    (DOWN_ALL, 3), (SIDE_ALL, 3), (FAR, 0), (UP_SIDE_1, 0), (OWN, 1), (DOWN_SIDE_2, 0), (FAR, 3), (UP_SIDE_1, 3),
+    (DOWN_SIDE_2, 3), (UP_SIDE_2, 0), (DOWN_SIDE_1, 0), (UP_SIDE_2, 3), (DOWN_SIDE_1, 3), (OWN, 2), (DOWN_2, 1),
+    (SIDE_1, 1), (UP_1, 1), (OWN, 4), (SIDE_2, 1), (DOWN_ALL, 1), (UP_ALL, 1), (FAR_SIDE_1, 0), (SIDE_ALL, 1),
+    (FAR_SIDE_1, 3), (OWN, 5), (UP_1, 2), (SIDE_1, 2), (DOWN_2, 2), (SIDE_2, 2), (UP_ALL, 2), (DOWN_ALL, 2),
+    (SIDE_ALL, 2), (SIDE_1, 4), (UP_SIDE_1, 1), (SIDE_2, 4), (SCALE, 0), (SCALE, 1), (SIDE_ALL, 4), (FAR, 1),
+    (UP_1, 4), (DOWN_2, 4), (UP_ALL, 4), (DOWN_ALL, 4), (SIDE_1, 5), (UP_SIDE_2, 1), (DOWN_SIDE_2, 1),
+    (DOWN_SIDE_1, 1), (SIDE_2, 5), (UP_1, 5), (DOWN_2, 5), (SIDE_ALL, 5), (UP_ALL, 5), (DOWN_ALL, 5), (SCALE, 8),
+    (SCALE, 9), (UP_SIDE_1, 2), (FAR, 2), (UP_SIDE_2, 2), (DOWN_SIDE_2, 2), (DOWN_SIDE_1, 2), (UP_SIDE_1, 4),
+    (DOWN_SIDE_2, 4), (SCALE, 6), (SCALE, 7), (UP_SIDE_2, 4), (DOWN_SIDE_1, 5), (SCALE, 2), (FAR, 4),
+    (DOWN_SIDE_1, 4), (UP_SIDE_1, 5), (FAR_SIDE_1, 1), (UP_BETWEEN, 5), (UP_SIDE_2, 5), (DOWN_SIDE_2, 5), (SCALE, 3),
+    (DOWN_BETWEEN, 5), (FAR, 5), (FAR_SIDE_1, 2), (SCALE, 14), (SCALE, 15), (SCALE, 10), (FAR_SIDE_1, 5),
+    (FAR_SIDE_2, 5), (SCALE, 11), (FAR_SIDE_1, 4), (FAR_BETWEEN, 5), (SCALE, 4), (SCALE, 5), (SCALE, 12), (SCALE, 13),
 )
 
 
@@ -189,6 +195,8 @@
 
     def copy(k, tag, origin, core):
         _, piece, target = plan[tag]
+        if k in WHOLE and tag > 22:
+            piece = ALL
         ref = part(k, origin, core, *pieces(k)[piece])
         return pltpu.make_async_remote_copy(
             src_ref=ref,
@@ -219,7 +227,7 @@
     def scale(b, dy, zs):
         if zs == 0:
             for k in range(3 * b, 3 * b + 3):
-                wait(k, *FROM_TWIN[dy])
+                wait(k, *(WHOLE_FROM_TWIN if k in WHOLE else FROM_TWIN)[dy])
         first, count = BATCHES[b]
         n, ys = PIECE[b], (y + dy) % NY
 
@@ -276,12 +284,14 @@
         elif step == SCALE:
             scale(k // 8, k // 2 % NY, k % 2)
         else:
-            wait(k, *STEPS[step][0])
-            send(k, *STEPS[step][1])
+            first, then = (WHOLE_STEPS if k in WHOLE else STEPS)[step]
+            wait(k, *first)
+            send(k, *then)
 
     for k, (b, kind) in enumerate(CHUNKS):
         for t in range(TAGS):
-            copy(k, t, plan[t][0], c).wait_send()
+            if k not in WHOLE or t < 23 or t in (23, 25, 27):
+                copy(k, t, plan[t][0], c).wait_send()
         lot = 3 if kind == SAME else SOURCES[kind]
         gone = part(k, chip(0, 0), c, 0, lot * PIECE[b])
         pltpu.make_async_copy(gone, gone, out_sem.at[b, k % 3]).wait()
@@ -290,10 +300,7 @@
 def place(slot_ref, buf, out_ref, scale_ref, found, sem, scale_sem):
     for s in range(EXPERTS):
         e = slot_ref[s]
-        for ch in range(CHIPS):
-            pltpu.make_async_copy(
-                buf.at[e, ch, pl.ds(0, SHARE)], out_ref.at[s, pl.ds(ch * SHARE, SHARE)], sem.at[s, ch]
-            ).start()
+        pltpu.make_async_copy(buf.at[e, :, pl.ds(0, SHARE)], out_ref.at[s], sem.at[s]).start()
     row = lax.broadcasted_iota(jnp.int32, (16, QB), 0)
     lane = lax.broadcasted_iota(jnp.int32, (16, QB), 1)
     lines = jnp.zeros((16, QB), jnp.float32)
@@ -309,10 +316,7 @@
     out = pltpu.make_async_copy(found, scale_ref, scale_sem)
     out.start()
     for s in range(EXPERTS):
-        for ch in range(CHIPS):
-            pltpu.make_async_copy(
-                buf.at[0, ch, pl.ds(0, SHARE)], out_ref.at[s, pl.ds(ch * SHARE, SHARE)], sem.at[s, ch]
-            ).wait()
+        pltpu.make_async_copy(buf.at[0, :, pl.ds(0, SHARE)], out_ref.at[s], sem.at[s]).wait()
     out.wait()
 
 
@@ -343,7 +347,7 @@
     placed, scales = pl.pallas_call(
         place,
         out_shape=(
-            jax.ShapeDtypeStruct((EXPERTS, CHIPS * SHARE, QB), jnp.bfloat16),
+            jax.ShapeDtypeStruct((EXPERTS, CHIPS, SHARE, QB), jnp.bfloat16),
             jax.ShapeDtypeStruct((EXPERTS, CHIPS * BLOCKS), jnp.bfloat16),
         ),
         in_specs=[
@@ -353,13 +357,13 @@
         out_specs=(pl.BlockSpec(memory_space=pl.ANY), pl.BlockSpec(memory_space=pl.ANY)),
         scratch_shapes=[
             pltpu.VMEM((EXPERTS, CHIPS * BLOCKS), jnp.bfloat16),
-            pltpu.SemaphoreType.DMA((EXPERTS, CHIPS)),
+            pltpu.SemaphoreType.DMA((EXPERTS,)),
             pltpu.SemaphoreType.DMA,
         ],
         compiler_params=pltpu.CompilerParams(vmem_limit_bytes=20 * 2**20),
         name="place",
     )(expert_of_slot, gathered)
-    return placed, scales.reshape(EXPERTS, CHIPS * BLOCKS, 1)
+    return placed.reshape(EXPERTS, CHIPS * SHARE, QB), scales.reshape(EXPERTS, CHIPS * BLOCKS, 1)
 
 
 def solution(mesh):

time: 66.9 us -> 66.3 us (level)
  Pallas kernels: 66.2 us -> 65.5 us
where the time goes in v4:
time: 66.3 us; the launch traced here: 66.2 us
  Pallas kernels  65.5 us (99%)
    pallas_call x1, Pallas kernels, shards(): pl.pallas_call(spread, out_shape=pltpu.VMEM((EXPERTS, CHIPS, SHARE + 16,...  60.8 us
    pallas_call x1, Pallas kernels, shards(): pl.pallas_call(place, out_shape=(jax.ShapeDtypeStruct((EXPERTS, CHIPS, SH...  4.75 us

profile of v4, /device:TPU:1, one launch (start us, length us, event | category | flops | bytes accessed | tf_op | source)
XLA Modules:
  0.0 66.2 jit_solution(12613920673574528419)
XLA Ops:
  0.6 0.0 copy-start
  0.6 60.8 %spread.1.buf = bf16[6,8,912,128]{3,2,1,0:T(8,128)(2,1)S(1)} custom-call(bf16[6,28,2048]{2,1,0:T(8,128)(2,1)} %x_ref.1), custom_call_target="tpu_custom_call" | custom-call | tf_op jit(solution)/shard_map/spread/pallas_call | solution.py:326
  61.4 0.0 copy-done
  61.4 4.8 %place.1 = (bf16[6,8,896,128]{3,2,1,0:T(8,128)(2,1)}, bf16[6,56]{1,0:T(8,128)(2,1)}) custom-call(s32[6]{0:T(128)S(1)} %copy-done, bf16[6,8,912,128]{3,2,1,0:T(8,128)(2,1)S(1)} %spread.1.buf), custom_call_target="tpu_custom_call" | custom-call | tf_op jit(solution)/shard_map/place/pallas_call | solution.py:347
Async XLA Ops:
  0.6 60.8 %copy-start = (s32[6]{0:T(128)S(1)}, s32[6]{0:T(128)}, u32[]{:S(2)}) copy-start(s32[6]{0:T(128)} %slot_ref.1) | copy-start | bytes 76

commit v5 on v4

--- a/solution.py
+++ b/solution.py
@@ -59,7 +59,7 @@
 }
 WHOLE_FROM_TWIN = ((18, 19), (21, 25), (22, 27), (20, 23))
 ORDER = (
-    (ROUND, 0), (OWN, 0), (OWN, 3), (ROUND, 1), (ROUND, 2), (UP_1, 0), (DOWN_2, 0), (SIDE_1, 0), (UP_ALL, 0),
+    (ROUND, 0), (OWN, 0), (ROUND, 1), (OWN, 3), (ROUND, 2), (UP_1, 0), (DOWN_2, 0), (SIDE_1, 0), (UP_ALL, 0),
     (SIDE_2, 0), (DOWN_ALL, 0), (SIDE_ALL, 0), (UP_1, 3), (DOWN_2, 3), (SIDE_1, 3), (UP_ALL, 3), (SIDE_2, 3),
     (DOWN_ALL, 3), (SIDE_ALL, 3), (FAR, 0), (UP_SIDE_1, 0), (OWN, 1), (DOWN_SIDE_2, 0), (FAR, 3), (UP_SIDE_1, 3),
     (DOWN_SIDE_2, 3), (UP_SIDE_2, 0), (DOWN_SIDE_1, 0), (UP_SIDE_2, 3), (DOWN_SIDE_1, 3), (OWN, 2), (DOWN_2, 1),

time: 66.3 us -> 66.5 us (level)
  no operation moved by 1% of the time
where the time goes in v5:
time: 66.5 us; the launch traced here: 66.4 us
  Pallas kernels  65.7 us (99%)
    pallas_call x1, Pallas kernels, shards(): pl.pallas_call(spread, out_shape=pltpu.VMEM((EXPERTS, CHIPS, SHARE + 16,...  60.9 us
    pallas_call x1, Pallas kernels, shards(): pl.pallas_call(place, out_shape=(jax.ShapeDtypeStruct((EXPERTS, CHIPS, SH...  4.75 us

profile of v5, /device:TPU:1, one launch (start us, length us, event | category | flops | bytes accessed | tf_op | source)
XLA Modules:
  0.0 66.4 jit_solution(2347099271398419138)
XLA Ops:
  0.6 0.0 copy-start
  0.6 60.9 %spread.1.buf = bf16[6,8,912,128]{3,2,1,0:T(8,128)(2,1)S(1)} custom-call(bf16[6,28,2048]{2,1,0:T(8,128)(2,1)} %x_ref.1), custom_call_target="tpu_custom_call" | custom-call | tf_op jit(solution)/shard_map/spread/pallas_call | solution.py:326
  61.6 0.0 copy-done
  61.6 4.8 %place.1 = (bf16[6,8,896,128]{3,2,1,0:T(8,128)(2,1)}, bf16[6,56]{1,0:T(8,128)(2,1)}) custom-call(s32[6]{0:T(128)S(1)} %copy-done, bf16[6,8,912,128]{3,2,1,0:T(8,128)(2,1)S(1)} %spread.1.buf), custom_call_target="tpu_custom_call" | custom-call | tf_op jit(solution)/shard_map/place/pallas_call | solution.py:347
Async XLA Ops:
  0.6 61.0 %copy-start = (s32[6]{0:T(128)S(1)}, s32[6]{0:T(128)}, u32[]{:S(2)}) copy-start(s32[6]{0:T(128)} %slot_ref.1) | copy-start | bytes 76
